TPU v7x, 256 devices: a whole 4x4x8 slice. The times are simulated.
256 devices in a mesh: section: 8 (over x, y_lo), seq: 32 (over z, y_hi, core).
Axes of the slice: x: 4, y: 4 (y_hi: 2, y_lo: 2; y = y_hi * 2 + y_lo), z: 8, core: 2. Of those that a mesh axis runs over, the one named last changes fastest.
Arguments:
- queries: bfloat16 [8, 4096, 4096], P('section', 'seq'), may hold values from -6 to 6
- key_rows: bfloat16 [8, 4096, 512], P('section', 'seq'), may hold values from -6 to 6
- value_rows: bfloat16 [8, 4096, 512], P('section', 'seq'), may hold values from -6 to 6
- upstream: bfloat16 [8, 4096, 4096], P('section', 'seq'), may hold values from -6 to 6
- norm_gains: float32 [8, 256], P('section'), may hold values from 0.5 to 8, as said below
- segments: int32 [8, 4096], P('section'), may hold values from 0 to 5, never falling along the last dimension, each value on 1 to 1024 neighbouring positions
Outputs:
- attended: bfloat16 [8, 4096, 4096], P('section', 'seq')
- grad_queries: bfloat16 [8, 4096, 4096], P('section', 'seq')
- grad_keys: bfloat16 [8, 4096, 512], P('section', 'seq')
- grad_values: bfloat16 [8, 4096, 512], P('section', 'seq')
- grad_gains: float32 [8, 256], P('section')
Inputs may be any that keep to these rules, and one draw needn't show every extreme that they name: `norm_gains`: row g of the gains equals row 7 - g. `segments`: document numbers never fall along a slab; a document spans at most 1024 tokens of it.
All inputs are finite; a program needn't handle non-finite values.
Results may differ from a plain program's by a relative error of at most 0.033.
The roundings to bfloat16 on the way count: a program that leaves them out, or rounds other values in their place, can miss the bound.
Values may be sent and summed in bfloat16 or wider, within the bound.
A program may use at most 128 MiB of HBM per device.

v0:
```python
import math

import jax
import jax.numpy as jnp
from jax import lax
from jax.sharding import PartitionSpec as P

SEQ_DEV = 64
HEAD_DIM = 128
KV_HEADS = 4


epsilon = 1e-06


def from_partner(block, axis, apart):
    count = lax.axis_size(axis)
    route = []
    for low in range(count):
        high = low | 1 << apart
        if high != low and high < count:
            route += [(low, high), (high, low)]
    return lax.ppermute(block, axis, route)


def unit_rows(raw):
    values_f = raw.astype(jnp.float32)
    root_mean = jnp.sqrt(jnp.mean(values_f * values_f, axis=-1, keepdims=True) + epsilon)
    return (values_f / root_mean, root_mean)


def attend_head(q_head, k_head, v_head, up_head, seg_ids, seq_len):
    total = q_head.shape[0]
    width = q_head.shape[1]
    block = min(512, seq_len)
    factor = 1.0 / math.sqrt(width)
    out_blocks = []
    dq_blocks = []
    dk_blocks = []
    dv_blocks = []
    for seq_id in range(total // seq_len):
        seq_first = seq_id * seq_len
        dk_acc = jnp.zeros((seq_len, width), jnp.float32)
        dv_acc = jnp.zeros((seq_len, width), jnp.float32)
        for block_id in range(seq_len // block):
            first = seq_first + block_id * block
            last = first + block
            span = last - seq_first
            q_block = q_head[first:last]
            up_block = up_head[first:last]
            k_seen = k_head[seq_first:last]
            v_seen = v_head[seq_first:last]
            scores = jnp.dot(q_block, k_seen.T, preferred_element_type=jnp.float32) * factor
            row_pos = block_id * block + jnp.arange(block, dtype=jnp.int32)[:, None]
            col_pos = jnp.arange(span, dtype=jnp.int32)[None, :]
            allowed = (col_pos <= row_pos) & (
                seg_ids[first:last][:, None] == seg_ids[seq_first:last][None, :]
            )
            scores = jnp.where(allowed, scores, -jnp.inf)
            top_score = jnp.max(scores, axis=1, keepdims=True)
            weights = jnp.exp(scores - top_score)
            probs = weights / jnp.sum(weights, axis=1, keepdims=True)
            probs_b = probs.astype(jnp.bfloat16)
            output_b = jnp.dot(probs_b, v_seen, preferred_element_type=jnp.float32).astype(
                jnp.bfloat16
            )
            delta = jnp.sum(
                up_block.astype(jnp.float32) * output_b.astype(jnp.float32), axis=1, keepdims=True
            )
            d_probs = jnp.dot(up_block, v_seen.T, preferred_element_type=jnp.float32)
            d_scores = (probs * (d_probs - delta) * factor).astype(jnp.bfloat16)
            dq_blocks.append(
                jnp.dot(d_scores, k_seen, preferred_element_type=jnp.float32).astype(jnp.bfloat16)
            )
            dk_part = jnp.dot(d_scores.T, q_block, preferred_element_type=jnp.float32)
            dv_part = jnp.dot(probs_b.T, up_block, preferred_element_type=jnp.float32)
            dk_acc = dk_acc + jnp.pad(dk_part, ((0, seq_len - span), (0, 0)))
            dv_acc = dv_acc + jnp.pad(dv_part, ((0, seq_len - span), (0, 0)))
            out_blocks.append(output_b)
        dk_blocks.append(dk_acc)
        dv_blocks.append(dv_acc)
    return (
        jnp.concatenate(out_blocks, 0),
        jnp.concatenate(dq_blocks, 0),
        jnp.concatenate(dk_blocks, 0),
        jnp.concatenate(dv_blocks, 0),
    )


def on_device(queries, key_rows, value_rows, upstream, norm_gains, segments):
    query_rows = queries[0]
    keys_local = key_rows[0]
    values_local = value_rows[0]
    upstream_rows = upstream[0]
    seg_ids = segments[0]
    row_count = query_rows.shape[0]
    head_count = query_rows.shape[1] // HEAD_DIM
    groups = head_count // KV_HEADS
    seq_len = SEQ_DEV * lax.axis_size("seq")
    gain_q = norm_gains[0, :HEAD_DIM]
    gain_k = norm_gains[0, HEAD_DIM:]
    q_unit, q_root = unit_rows(query_rows.reshape(row_count, head_count, HEAD_DIM))
    k_unit, k_root = unit_rows(keys_local.reshape(row_count, KV_HEADS, HEAD_DIM))
    q_normed = (q_unit * gain_q).astype(jnp.bfloat16).reshape(row_count, head_count * HEAD_DIM)
    k_normed = (k_unit * gain_k).astype(jnp.bfloat16)
    k_copies = jnp.broadcast_to(
        k_normed[:, :, None, :], (row_count, KV_HEADS, groups, HEAD_DIM)
    ).reshape(row_count, head_count * HEAD_DIM)
    v_shaped = values_local.reshape(row_count, KV_HEADS, HEAD_DIM)
    v_copies = jnp.broadcast_to(
        v_shaped[:, :, None, :], (row_count, KV_HEADS, groups, HEAD_DIM)
    ).reshape(row_count, head_count * HEAD_DIM)
    q_heads, k_heads, v_heads, up_heads = (
        lax.all_to_all(q_normed, "seq", split_axis=1, concat_axis=0, tiled=True),
        lax.all_to_all(k_copies, "seq", split_axis=1, concat_axis=0, tiled=True),
        lax.all_to_all(v_copies, "seq", split_axis=1, concat_axis=0, tiled=True),
        lax.all_to_all(upstream_rows, "seq", split_axis=1, concat_axis=0, tiled=True),
    )
    out_b, dq_b, dk_f, dv_f = attend_head(q_heads, k_heads, v_heads, up_heads, seg_ids, seq_len)
    out_rows, dq_rows = (
        lax.all_to_all(out_b, "seq", split_axis=0, concat_axis=1, tiled=True),
        lax.all_to_all(dq_b, "seq", split_axis=0, concat_axis=1, tiled=True),
    )
    dk_rows, dv_rows = (
        lax.all_to_all(
            dk_f.astype(jnp.bfloat16), "seq", split_axis=0, concat_axis=1, tiled=True
        ).astype(dk_f.dtype),
        lax.all_to_all(
            dv_f.astype(jnp.bfloat16), "seq", split_axis=0, concat_axis=1, tiled=True
        ).astype(dv_f.dtype),
    )
    dk_sum = dk_rows.reshape(row_count, KV_HEADS, groups, HEAD_DIM).sum(axis=2)
    dv_sum = dv_rows.reshape(row_count, KV_HEADS, groups, HEAD_DIM).sum(axis=2)
    d_qn = dq_rows.astype(jnp.float32).reshape(row_count, head_count, HEAD_DIM)
    scaled_q = d_qn * gain_q
    grad_q = (
        (scaled_q - q_unit * jnp.mean(scaled_q * q_unit, axis=-1, keepdims=True)) / q_root
    ).astype(jnp.bfloat16)
    scaled_k = dk_sum * gain_k
    grad_k = (
        (scaled_k - k_unit * jnp.mean(scaled_k * k_unit, axis=-1, keepdims=True)) / k_root
    ).astype(jnp.bfloat16)
    local_terms = jnp.concatenate(
        [jnp.sum(d_qn * q_unit, axis=(0, 1)), jnp.sum(dk_sum * k_unit, axis=(0, 1))]
    )
    group_terms = lax.psum(local_terms, "seq")
    mirrored = group_terms
    for bit_pos in range(lax.axis_size("section").bit_length() - 1):
        mirrored = from_partner(mirrored, "section", bit_pos)
    grad_gains = group_terms + mirrored
    return (
        out_rows[None],
        grad_q.reshape(row_count, head_count * HEAD_DIM)[None],
        grad_k.reshape(row_count, KV_HEADS * HEAD_DIM)[None],
        dv_sum.astype(jnp.bfloat16).reshape(row_count, KV_HEADS * HEAD_DIM)[None],
        grad_gains[None],
    )


def solution(mesh):
    return jax.shard_map(
        on_device,
        mesh=mesh,
        in_specs=(
            P("section", "seq", None),
            P("section", "seq", None),
            P("section", "seq", None),
            P("section", "seq", None),
            P("section", None),
            P("section", None),
        ),
        out_specs=(
            P("section", "seq", None),
            P("section", "seq", None),
            P("section", "seq", None),
            P("section", "seq", None),
            P("section", None),
        ),
        check_vma=False,
    )
```

profile of v0, /device:TPU:1, one launch (start us, length us, event | category | flops | bytes accessed | tf_op | source)
XLA Modules:
  0.0 396.9 jit_solution(440891138879821369)
XLA Ops:
  4.0 12.8 %all-to-all-start.1 = ((bf16[128,32,128]{2,0,1:T(8,128)(2,1)}), bf16[128,32,128]{2,0,1:T(8,128)(2,1)S(1)}, u32[]{:S(2)}, u32[]{:S(2)}) async-start(bf16[128,32,128]{2,0,1:T(8,128)(2,1)} %bitcast.8), calls=%async_computation.1 | async-start | bytes 2097152 | tf_op jit(solution)/shard_map/all_to_all | solution.py:115
  16.9 28.0 %all-to-all-done.1 = bf16[128,32,128]{2,0,1:T(8,128)(2,1)S(1)} async-done(((bf16[128,32,128]{2,0,1:T(8,128)(2,1)}), bf16[128,32,128]{2,0,1:T(8,128)(2,1)S(1)}, u32[]{:S(2)}, u32[]{:S(2)}) %all-to-all-start.1) | async-done | bytes 1048608 | tf_op jit(solution)/shard_map/all_to_all | solution.py:115
  46.1 5.8 %all-to-all-start.2 = ((bf16[128,32,128]{2,0,1:T(8,128)(2,1)}), bf16[128,32,128]{2,0,1:T(8,128)(2,1)S(1)}, u32[]{:S(2)}, u32[]{:S(2)}) async-start(bf16[128,32,128]{2,0,1:T(8,128)(2,1)} %bitcast.11), calls=%async_computation.2 | async-start | bytes 2097152 | tf_op jit(solution)/shard_map/all_to_all | solution.py:116
  51.9 1.6 copy.127
  55.2 24.9 %all-to-all-done.2 = bf16[128,32,128]{2,0,1:T(8,128)(2,1)S(1)} async-done(((bf16[128,32,128]{2,0,1:T(8,128)(2,1)}), bf16[128,32,128]{2,0,1:T(8,128)(2,1)S(1)}, u32[]{:S(2)}, u32[]{:S(2)}) %all-to-all-start.2) | async-done | bytes 1048608 | tf_op jit(solution)/shard_map/all_to_all | solution.py:116
  80.0 5.8 %all-to-all-start = ((bf16[128,32,128]{0,2,1:T(8,128)(2,1)}), bf16[128,32,128]{0,2,1:T(8,128)(2,1)}, u32[]{:S(2)}, u32[]{:S(2)}) async-start(bf16[128,32,128]{0,2,1:T(8,128)(2,1)} %multiply_convert_fusion.4), calls=%async_computation | async-start | bytes 2097152 | tf_op jit(solution)/shard_map/all_to_all | solution.py:114
  93.0 21.1 %all-to-all-done = bf16[128,32,128]{0,2,1:T(8,128)(2,1)} async-done(((bf16[128,32,128]{0,2,1:T(8,128)(2,1)}), bf16[128,32,128]{0,2,1:T(8,128)(2,1)}, u32[]{:S(2)}, u32[]{:S(2)}) %all-to-all-start) | async-done | bytes 1048608 | tf_op jit(solution)/shard_map/all_to_all | solution.py:114
  114.1 6.4 %all-to-all-start.4 = ((bf16[128,32,128]{2,0,1:T(8,128)(2,1)}), bf16[128,32,128]{2,0,1:T(8,128)(2,1)}, u32[]{:S(2)}, u32[]{:S(2)}) async-start(bf16[128,32,128]{2,0,1:T(8,128)(2,1)} %copy.142), calls=%async_computation.4 | async-start | bytes 2097152 | tf_op jit(solution)/shard_map/all_to_all | solution.py:117
  120.4 2.1 fusion.82
  122.6 1.7 copy.140
  124.2 1.7 copy.139
  125.9 1.7 copy.138
  127.5 1.7 copy.137
  129.2 1.6 copy.136
  140.1 8.0 %all-to-all-done.4 = bf16[128,32,128]{2,0,1:T(8,128)(2,1)} async-done(((bf16[128,32,128]{2,0,1:T(8,128)(2,1)}), bf16[128,32,128]{2,0,1:T(8,128)(2,1)}, u32[]{:S(2)}, u32[]{:S(2)}) %all-to-all-start.4) | async-done | bytes 1048608 | tf_op jit(solution)/shard_map/all_to_all | solution.py:117
  181.8 1.5 fusion.106
  190.3 6.0 %all-to-all-start.7 = ((bf16[32,128,128]{2,1,0:T(8,128)(2,1)}), bf16[32,128,128]{2,1,0:T(8,128)(2,1)}, u32[]{:S(2)}, u32[]{:S(2)}) async-start(bf16[32,128,128]{2,1,0:T(8,128)(2,1)} %bitcast.228), calls=%async_computation.7 | async-start | bytes 2097152 | tf_op jit(solution)/shard_map/all_to_all | solution.py:128
  196.3 3.7 constant_dynamic-update-slice_fusion
  209.6 14.9 %all-to-all-done.7 = bf16[32,128,128]{2,1,0:T(8,128)(2,1)} async-done(((bf16[32,128,128]{2,1,0:T(8,128)(2,1)}), bf16[32,128,128]{2,1,0:T(8,128)(2,1)}, u32[]{:S(2)}, u32[]{:S(2)}) %all-to-all-start.7) | async-done | bytes 1048608 | tf_op jit(solution)/shard_map/all_to_all | solution.py:128
  224.5 6.4 %all-to-all-start.6 = ((bf16[32,128,128]{2,1,0:T(8,128)(2,1)}), bf16[32,128,128]{2,1,0:T(8,128)(2,1)}, u32[]{:S(2)}, u32[]{:S(2)}) async-start(bf16[32,128,128]{2,1,0:T(8,128)(2,1)} %bitcast.227), calls=%async_computation.6 | async-start | bytes 2097152 | tf_op jit(solution)/shard_map/all_to_all | solution.py:125
  232.3 1.8 fusion.50
  239.3 2.2 copy.145
  241.6 17.3 %all-to-all-done.6 = bf16[32,128,128]{2,1,0:T(8,128)(2,1)} async-done(((bf16[32,128,128]{2,1,0:T(8,128)(2,1)}), bf16[32,128,128]{2,1,0:T(8,128)(2,1)}, u32[]{:S(2)}, u32[]{:S(2)}) %all-to-all-start.6) | async-done | bytes 1048608 | tf_op jit(solution)/shard_map/all_to_all | solution.py:125
  258.9 5.8 %all-to-all-start.5 = ((bf16[32,128,128]{1,2,0:T(8,128)(2,1)}), bf16[32,128,128]{1,2,0:T(8,128)(2,1)S(1)}, u32[]{:S(2)}, u32[]{:S(2)}) async-start(bf16[32,128,128]{1,2,0:T(8,128)(2,1)} %copy.145), calls=%async_computation.5 | async-start | bytes 2097152 | tf_op jit(solution)/shard_map/all_to_all | solution.py:122
  265.3 27.5 %all-to-all-done.5 = bf16[32,128,128]{1,2,0:T(8,128)(2,1)S(1)} async-done(((bf16[32,128,128]{1,2,0:T(8,128)(2,1)}), bf16[32,128,128]{1,2,0:T(8,128)(2,1)S(1)}, u32[]{:S(2)}, u32[]{:S(2)}) %all-to-all-start.5) | async-done | bytes 1048608 | tf_op jit(solution)/shard_map/all_to_all | solution.py:122
  292.8 5.9 %all-to-all-start.3 = ((bf16[32,128,128]{2,1,0:T(8,128)(2,1)}), bf16[32,128,128]{2,1,0:T(8,128)(2,1)S(1)}, u32[]{:S(2)}, u32[]{:S(2)}) async-start(bf16[32,128,128]{2,1,0:T(8,128)(2,1)} %bitcast.257), calls=%async_computation.3 | async-start | bytes 2097152 | tf_op jit(solution)/shard_map/all_to_all | solution.py:121
  298.8 2.1 bitcast_reduce_fusion
  300.9 1.8 copy.146
  306.5 75.4 %psum.7 = f32[256]{0:T(256)S(1)} all-reduce(f32[256]{0:T(256)S(1)} %pad_maximum_fusion.2), channel_id=1, replica_groups=mesh['section'=8,'seq'=32] {'seq'}, use_global_device_ids=true, to_apply=%region_33.34 | all-reduce | flops 256 | bytes 2048 | tf_op jit(solution)/shard_map/psum | solution.py:146
  382.4 2.0 collective-permute-done
  385.7 1.6 fusion.29
  387.3 2.5 collective-permute-start.2
  (301 shorter events, 91.5 us)
Async XLA Ops:
  1.7 15.1 %copy-start.65 = (bf16[1,128,512]{2,1,0:T(8,128)(2,1)S(1)}, bf16[1,128,512]{2,1,0:T(8,128)(2,1)}, u32[]{:S(2)}) copy-start(bf16[1,128,512]{2,1,0:T(8,128)(2,1)} %param.8) | copy-start | bytes 393220
  1.8 15.0 %copy-start.20 = (f32[128,4,128]{2,0,1:T(8,128)}, f32[128,4,128]{2,0,1:T(8,128)S(1)}, u32[]{:S(2)}) copy-start(f32[128,4,128]{2,0,1:T(8,128)S(1)} %copy.132) | copy-start | bytes 786436
  2.6 14.2 %copy-start.68 = (f32[128]{0:T(128)}, f32[128]{0:T(128)S(1)}, u32[]{:S(2)}) copy-start(f32[128]{0:T(128)S(1)} %get-tuple-element.80) | copy-start | bytes 1540
  2.6 51.2 %copy-start.74 = (f32[128]{0:T(128)}, f32[128]{0:T(128)S(1)}, u32[]{:S(2)}) copy-start(f32[128]{0:T(128)S(1)} %get-tuple-element.81) | copy-start | bytes 1540
  2.6 14.2 %copy-start.66 = (f32[128,4]{0,1:T(4,128)}, f32[128,4]{0,1:T(4,128)S(1)}, u32[]{:S(2)}) copy-start(f32[128,4]{0,1:T(4,128)S(1)} %add_sqrt_fusion.1) | copy-start | bytes 6148
  4.0 40.9 %all-to-all-start.1 = ((bf16[128,32,128]{2,0,1:T(8,128)(2,1)}), bf16[128,32,128]{2,0,1:T(8,128)(2,1)S(1)}, u32[]{:S(2)}, u32[]{:S(2)}) async-start(bf16[128,32,128]{2,0,1:T(8,128)(2,1)} %bitcast.8), calls=%async_computation.1 | async-start | bytes 2097152 | tf_op jit(solution)/shard_map/all_to_all | solution.py:115
  46.1 33.9 %all-to-all-start.2 = ((bf16[128,32,128]{2,0,1:T(8,128)(2,1)}), bf16[128,32,128]{2,0,1:T(8,128)(2,1)S(1)}, u32[]{:S(2)}, u32[]{:S(2)}) async-start(bf16[128,32,128]{2,0,1:T(8,128)(2,1)} %bitcast.11), calls=%async_computation.2 | async-start | bytes 2097152 | tf_op jit(solution)/shard_map/all_to_all | solution.py:116
  80.0 34.0 %all-to-all-start = ((bf16[128,32,128]{0,2,1:T(8,128)(2,1)}), bf16[128,32,128]{0,2,1:T(8,128)(2,1)}, u32[]{:S(2)}, u32[]{:S(2)}) async-start(bf16[128,32,128]{0,2,1:T(8,128)(2,1)} %multiply_convert_fusion.4), calls=%async_computation | async-start | bytes 2097152 | tf_op jit(solution)/shard_map/all_to_all | solution.py:114
  114.1 34.0 %all-to-all-start.4 = ((bf16[128,32,128]{2,0,1:T(8,128)(2,1)}), bf16[128,32,128]{2,0,1:T(8,128)(2,1)}, u32[]{:S(2)}, u32[]{:S(2)}) async-start(bf16[128,32,128]{2,0,1:T(8,128)(2,1)} %copy.142), calls=%async_computation.4 | async-start | bytes 2097152 | tf_op jit(solution)/shard_map/all_to_all | solution.py:117
  139.1 10.4 %copy-start.52 = (bf16[4,128,128]{2,1,0:T(8,128)(2,1)S(1)}, bf16[4,128,128]{2,1,0:T(8,128)(2,1)}, u32[]{:S(2)}) copy-start(bf16[4,128,128]{2,1,0:T(8,128)(2,1)} %copy.130) | copy-start | bytes 393220
  139.1 10.4 %copy-start.61 = (bf16[4,128,128]{2,1,0:T(8,128)(2,1)S(1)}, bf16[4,128,128]{2,1,0:T(8,128)(2,1)}, u32[]{:S(2)}) copy-start(bf16[4,128,128]{2,1,0:T(8,128)(2,1)} %get-tuple-element.65) | copy-start | bytes 393220
  139.1 10.4 %copy-start.85 = (s32[1,512]{1,0:T(1,128)S(1)}, s32[1,512]{1,0:T(1,128)}, u32[]{:S(2)}) copy-start(s32[1,512]{1,0:T(1,128)} %get-tuple-element.75) | copy-start | bytes 6148
  149.5 36.9 %copy-start.31 = (bf16[4,128,128]{2,1,0:T(8,128)(2,1)}, bf16[4,128,128]{2,1,0:T(8,128)(2,1)S(1)}, u32[]{:S(2)}) copy-start(bf16[4,128,128]{2,1,0:T(8,128)(2,1)S(1)} %get-tuple-element.38) | copy-start | bytes 393220
  149.5 37.7 %copy-start.24 = (bf16[4,128,128]{2,1,0:T(8,128)(2,1)}, bf16[4,128,128]{2,1,0:T(8,128)(2,1)S(1)}, u32[]{:S(2)}) copy-start(bf16[4,128,128]{2,1,0:T(8,128)(2,1)S(1)} %get-tuple-element.34) | copy-start | bytes 393220
  172.8 13.6 %copy-start = (f32[512,2048]{1,0:T(8,128)}, f32[512,2048]{1,0:T(8,128)S(1)}, u32[]{:S(2)}) copy-start(f32[512,2048]{1,0:T(8,128)S(1)} %fusion.2) | copy-start | bytes 12582916
  189.2 7.1 %copy-start.13 = (bf16[16,128,128]{2,1,0:T(8,128)(2,1)S(1)}, bf16[16,128,128]{2,1,0:T(8,128)(2,1)}, u32[]{:S(2)}) copy-start(bf16[16,128,128]{2,1,0:T(8,128)(2,1)} %get-tuple-element.52) | copy-start | bytes 1572868
  190.3 9.8 %copy-start.49 = (bf16[4,128,128]{2,1,0:T(8,128)(2,1)S(1)}, bf16[4,128,128]{2,1,0:T(8,128)(2,1)}, u32[]{:S(2)}) copy-start(bf16[4,128,128]{2,1,0:T(8,128)(2,1)} %copy.137) | copy-start | bytes 393220
  190.3 34.2 %all-to-all-start.7 = ((bf16[32,128,128]{2,1,0:T(8,128)(2,1)}), bf16[32,128,128]{2,1,0:T(8,128)(2,1)}, u32[]{:S(2)}, u32[]{:S(2)}) async-start(bf16[32,128,128]{2,1,0:T(8,128)(2,1)} %bitcast.228), calls=%async_computation.7 | async-start | bytes 2097152 | tf_op jit(solution)/shard_map/all_to_all | solution.py:128
  196.3 5.3 %copy-start.1 = (f32[512,2048]{1,0:T(8,128)S(1)}, f32[512,2048]{1,0:T(8,128)}, u32[]{:S(2)}) copy-start(f32[512,2048]{1,0:T(8,128)} %copy-done) | copy-start | bytes 12582916
  196.3 5.3 %copy-start.15 = (bf16[16,128,128]{2,1,0:T(8,128)(2,1)S(1)}, bf16[16,128,128]{2,1,0:T(8,128)(2,1)}, u32[]{:S(2)}) copy-start(bf16[16,128,128]{2,1,0:T(8,128)(2,1)} %get-tuple-element.53) | copy-start | bytes 1572868
  208.5 22.4 %copy-start.27 = (bf16[512,512]{0,1:T(8,128)(2,1)S(1)}, bf16[512,512]{0,1:T(8,128)(2,1)}, u32[]{:S(2)}) copy-start(bf16[512,512]{0,1:T(8,128)(2,1)} %copy-done.26) | copy-start | bytes 1572868
  224.5 9.6 %copy-start.38 = (bf16[12,128,128]{2,1,0:T(8,128)(2,1)S(1)}, bf16[12,128,128]{2,1,0:T(8,128)(2,1)}, u32[]{:S(2)}) copy-start(bf16[12,128,128]{2,1,0:T(8,128)(2,1)} %get-tuple-element.55) | copy-start | bytes 1179652
  224.5 34.4 %all-to-all-start.6 = ((bf16[32,128,128]{2,1,0:T(8,128)(2,1)}), bf16[32,128,128]{2,1,0:T(8,128)(2,1)}, u32[]{:S(2)}, u32[]{:S(2)}) async-start(bf16[32,128,128]{2,1,0:T(8,128)(2,1)} %bitcast.227), calls=%async_computation.6 | async-start | bytes 2097152 | tf_op jit(solution)/shard_map/all_to_all | solution.py:125
  239.3 25.4 %copy-start.69 = (f32[128]{0:T(128)S(1)}, f32[128]{0:T(128)}, u32[]{:S(2)}) copy-start(f32[128]{0:T(128)} %copy-done.68) | copy-start | bytes 1540
  258.9 34.0 %all-to-all-start.5 = ((bf16[32,128,128]{1,2,0:T(8,128)(2,1)}), bf16[32,128,128]{1,2,0:T(8,128)(2,1)S(1)}, u32[]{:S(2)}, u32[]{:S(2)}) async-start(bf16[32,128,128]{1,2,0:T(8,128)(2,1)} %copy.145), calls=%async_computation.5 | async-start | bytes 2097152 | tf_op jit(solution)/shard_map/all_to_all | solution.py:122
  264.7 37.9 %copy-start.21 = (f32[128,4,128]{2,0,1:T(8,128)S(1)}, f32[128,4,128]{2,0,1:T(8,128)}, u32[]{:S(2)}) copy-start(f32[128,4,128]{2,0,1:T(8,128)} %copy-done.20) | copy-start | bytes 786436
  292.8 11.1 %copy-start.34 = (bf16[1,128,512]{1,2,0:T(8,128)(2,1)S(1)}, bf16[1,128,512]{1,2,0:T(8,128)(2,1)}, u32[]{:S(2)}) copy-start(bf16[1,128,512]{1,2,0:T(8,128)(2,1)} %copy-done.33) | copy-start | bytes 393220
  292.8 99.2 %all-to-all-start.3 = ((bf16[32,128,128]{2,1,0:T(8,128)(2,1)}), bf16[32,128,128]{2,1,0:T(8,128)(2,1)S(1)}, u32[]{:S(2)}, u32[]{:S(2)}) async-start(bf16[32,128,128]{2,1,0:T(8,128)(2,1)} %bitcast.257), calls=%async_computation.3 | async-start | bytes 2097152 | tf_op jit(solution)/shard_map/all_to_all | solution.py:121
  303.9 81.8 %copy-start.75 = (f32[128]{0:T(128)S(1)}, f32[128]{0:T(128)}, u32[]{:S(2)}) copy-start(f32[128]{0:T(128)} %copy-done.74) | copy-start | bytes 1540
  382.0 2.5 collective-permute-start
  384.5 2.8 collective-permute-start.1
  387.3 8.8 %collective-permute-start.2 = (f32[256]{0:T(256)S(1)}, f32[256]{0:T(256)S(1)}, u32[]{:S(2)}, u32[]{:S(2)}) collective-permute-start(f32[256]{0:T(256)S(1)} %collective-permute-done.1), channel_id=1, source_target_pairs={{0,128},{128,0},{32,160},{160,32},{64,192},{192,64},{96,224},{224,... | collective-permute-start | bytes 3080 | tf_op jit(solution)/shard_map/ppermute | solution.py:23
  (68 other events, 115.7 us)
where the time goes:
time: 404 us; the launch traced here: 397 us
  waiting for transfers between devices  144 us (36%)
  blocking collectives  75.4 us (19%)
  starting transfers between devices  59 us (15%)
  local copies, waits for them, and re-layouts  51.6 us (13%)
  matrix products  39.9 us (10%)
  other arithmetic  25 us (6%)
    psum x1, blocking collectives, on_device(): group_terms = lax.psum(local_terms, 'seq')  75.4 us
    all_to_all x1, waiting for transfers between devices, on_device(): lax.all_to_all(k_copies, 'seq', split_axis=1, concat_axis=0, tiled=True)  28 us
    all_to_all x1, waiting for transfers between devices, on_device(): lax.all_to_all(dq_b, 'seq', split_axis=0, concat_axis=1, tiled=True)  27.5 us
    all_to_all x1, waiting for transfers between devices, on_device(): lax.all_to_all(v_copies, 'seq', split_axis=1, concat_axis=0, tiled=True)  24.9 us
    all_to_all x1, waiting for transfers between devices, on_device(): lax.all_to_all(q_normed, 'seq', split_axis=1, concat_axis=0, tiled=True)  21.1 us
    all_to_all x1, waiting for transfers between devices, on_device(): lax.all_to_all(dk_f.astype(jnp.bfloat16), 'seq', split_axis=0, concat_axi...  17.3 us
    unnamed x184, local copies, waits for them, and re-layouts  16.7 us
    all_to_all x1, waiting for transfers between devices, on_device(): lax.all_to_all(dv_f.astype(jnp.bfloat16), 'seq', split_axis=0, concat_axi...  14.9 us
  transfers between devices with their start and end apart: 11, of which 8 were waited for; matrix products, arithmetic and copies ran while one was open for 16% of the time, Pallas kernels for 0%

commit v1 on v0

v1 whole, which is shorter than its diff:
```python
import functools
import math

import jax
import jax.numpy as jnp
from jax import lax
from jax.experimental import pallas as pl
from jax.experimental.pallas import tpu as pltpu
from jax.sharding import PartitionSpec as P

MESH = pl.DeviceIdType.MESH
HEAD_DIM = 128
GROUP = 8
ROWS = 128
PAIR = 2 * ROWS
SLOTS = 5
SPAN = SLOTS * PAIR
SEEN = SPAN - ROWS
EPSILON = 1e-06
FACTOR = 1.0 / math.sqrt(HEAD_DIM)
EXP2_FACTOR = FACTOR * math.log2(math.e)
MASKED = -1e30
F32 = jnp.float32
BF16 = jnp.bfloat16


def matmul(left, right, left_dim, right_dim):
    return lax.dot_general(
        left, right, (((left_dim,), (right_dim,)), ((), ())), preferred_element_type=F32
    )


def unit_rows(raw):
    values = raw.astype(F32)
    inverse = lax.rsqrt(jnp.mean(values * values, axis=-1, keepdims=True) + EPSILON)
    return values * inverse, inverse


def at_slot(slot):
    return pl.ds(pl.multiple_of(slot * PAIR, PAIR), PAIR)


def kernel(
    queries, keys, values, upstream, gains, segments,
    attended, grad_q, grad_k, grad_v, grad_gains,
    q_raw, up_raw, kv_raw, k_normed, k_unit_t, bias, acc,
    out_stage, kv_stage, y_out, z_out, y_in, z_in, gain_acc, gain_a, gain_b,
    local_sem, core_send, core_recv, gather_send, gather_recv,
    reduce_send, reduce_recv, out_sem, out_send, out_recv,
    kv_sem, kv_send, kv_recv, ga_send, ga_recv, gb_send, gb_recv,
):
    section = lax.axis_index("section")
    place = lax.axis_index("seq")
    core = place % 2
    col = (place // 2) % 2
    z = place // 4
    mirror = section // 4
    z_count = 8

    def device(z_at, col_at, core_at, section_at=None):
        return (section if section_at is None else section_at, (z_at * 2 + col_at) * 2 + core_at)

    sibling = device(z, col, 1 - core)
    across = device(z, 1 - col, core)
    up_z = device((z + 1) % z_count, col, core)
    down_z = device((z + z_count - 1) % z_count, col, core)

    def z_peer(step):
        return device((z + step) % z_count, col, core)

    def square_peer(code):
        flip_m, flip_h, flip_c = code // 4, (code // 2) % 2, code % 2
        return device(
            z,
            1 - col if flip_h else col,
            1 - core if flip_c else core,
            7 - section if flip_m else section,
        )

    barrier = pltpu.get_barrier_semaphore()
    for step in range(1, 8):
        pl.semaphore_signal(barrier, inc=1, device_id=z_peer(step), device_id_type=MESH)
        pl.semaphore_signal(barrier, inc=1, device_id=square_peer(step), device_id_type=MESH)

    def remote(src, dst, send, recv, target):
        return pltpu.make_async_remote_copy(
            src_ref=src, dst_ref=dst, send_sem=send, recv_sem=recv,
            device_id=target, device_id_type=MESH,
        )

    def q_columns(core_at, j):
        return pl.ds(pl.multiple_of(core_at * 2048 + j * 1024, 1024), 1024)

    def kv_columns(core_at, j):
        return pl.ds(pl.multiple_of(core_at * 256 + j * 128, 128), 128)

    def token_rows(core_at):
        return pl.ds(pl.multiple_of((SLOTS - 1) * PAIR + core_at * ROWS, ROWS), ROWS)

    def own_copy(kind, j):
        if kind < 2:
            source = (keys, values)[kind]
            return pltpu.make_async_copy(
                source.at[0, :, kv_columns(core, j)],
                kv_raw.at[j, kind, token_rows(core), :],
                local_sem.at[kind, j],
            )
        source, target = ((queries, q_raw), (upstream, up_raw))[kind - 2]
        return pltpu.make_async_copy(
            source.at[0, :, q_columns(core, j)],
            target.at[core, :, pl.ds(pl.multiple_of(j * 1024, 1024), 1024)],
            local_sem.at[kind, j],
        )

    def core_copy(kind, j):
        if kind < 2:
            source = (keys, values)[kind]
            return remote(
                source.at[0, :, kv_columns(1 - core, j)],
                kv_raw.at[j, kind, token_rows(core), :],
                core_send.at[kind, j],
                core_recv.at[kind, j],
                sibling,
            )
        source, target = ((queries, q_raw), (upstream, up_raw))[kind - 2]
        return remote(
            source.at[0, :, q_columns(1 - core, j)],
            target.at[core, :, pl.ds(pl.multiple_of(j * 1024, 1024), 1024)],
            core_send.at[kind, j],
            core_recv.at[kind, j],
            sibling,
        )

    def gather_copy(j, step):
        if step < 2:
            source, landing, target = 4 - 2 * step, 2 - 2 * step, up_z
        else:
            source, landing, target = 4 - 2 * (step - 2 + col), 3 - 2 * (step - 2), across
        return remote(
            kv_raw.at[j, :, at_slot(source), :],
            kv_raw.at[j, :, at_slot(landing), :],
            gather_send.at[j, step],
            gather_recv.at[j, step],
            target,
        )

    for j in range(2):
        for kind in range(2):
            own_copy(kind, j).start()
    for j in range(2):
        for kind in range(2, 4):
            own_copy(kind, j).start()
    pl.semaphore_wait(barrier, 14)
    for j in range(2):
        for kind in range(2):
            core_copy(kind, j).start()
    for j in range(2):
        for kind in range(2, 4):
            core_copy(kind, j).start()

    pair_at = z * 2 + col
    pieces = []
    for piece in range(SPAN // 128):
        at = jnp.maximum(pair_at * 2 - 8 + piece, 0)
        pieces.append(segments[:, pl.ds(pl.multiple_of(at * 128, 128), 128)].astype(F32))
    row_at = lax.broadcasted_iota(jnp.int32, (ROWS, SEEN), 0)
    key_at = lax.broadcasted_iota(jnp.int32, (ROWS, SEEN), 1)
    diagonal = lax.broadcasted_iota(jnp.int32, (ROWS, ROWS), 0) == lax.broadcasted_iota(
        jnp.int32, (ROWS, ROWS), 1
    )
    for r in range(2):
        row_segments = jnp.sum(jnp.where(diagonal, pieces[8 + r], 0.0), axis=1, keepdims=True)
        key_segments = jnp.concatenate(pieces[r : r + 9], axis=1)
        first_key = 1024 - r * ROWS - (pair_at % 8) * PAIR
        allowed = (
            (key_at <= row_at + 1024) & (key_at >= first_key) & (key_segments == row_segments)
        )
        bias[r] = jnp.where(allowed, 0.0, MASKED)

    acc[...] = jnp.zeros_like(acc)
    gain_acc[...] = jnp.zeros_like(gain_acc)

    for j in range(2):
        for kind in range(2):
            own_copy(kind, j).wait()
            core_copy(kind, j).wait_recv()
        gather_copy(j, 0).start()

        @pl.when(col == 0)
        def _():
            gather_copy(j, 2).start()

    for j in range(2):
        gather_copy(j, 0).wait_recv()
        gather_copy(j, 1).start()

        @pl.when(col == 0)
        def _():
            gather_copy(j, 3).start()

        @pl.when(col == 1)
        def _():
            gather_copy(j, 2).start()

    for j in range(2):
        gather_copy(j, 1).wait_recv()

        @pl.when(col == 1)
        def _():
            gather_copy(j, 3).start()

    gain_q = gains[:, :HEAD_DIM]
    gain_k = gains[:, HEAD_DIM:]

    def reduce_copy(j, step):
        if step < 2:
            buffer_out, buffer_in, target = z_out.at[j, step], z_in.at[j, step], down_z
        else:
            buffer_out, buffer_in, target = y_out.at[j, step - 2], y_in.at[j, step - 2], across
        return remote(
            buffer_out, buffer_in, reduce_send.at[j, step], reduce_recv.at[j, step], target
        )

    def send_sum(j, step, slot):
        if step < 2:
            z_out[j, step] = acc[j, :, :, at_slot(slot)].astype(BF16)
        else:
            y_out[j, step - 2] = acc[j, :, :, at_slot(slot)].astype(BF16)
        reduce_copy(j, step).start()

    def add_sum(j, step, slot):
        reduce_copy(j, step).wait_recv()
        term = z_in[j, step] if step < 2 else y_in[j, step - 2]
        acc[j, :, :, at_slot(slot)] += term.astype(F32)

    def reduce_first(j):
        send_sum(j, 3, 1)
        send_sum(j, 2, 3)

        @pl.when(col == 0)
        def _():
            send_sum(j, 0, 0)

    def reduce_second(j):
        add_sum(j, 3, 2 * (1 - col))

        @pl.when(col == 1)
        def _():
            send_sum(j, 0, 0)

    def reduce_third(j):
        add_sum(j, 2, 4 - 2 * col)
        add_sum(j, 0, 2)
        send_sum(j, 1, 2)

    def kv_copy(kind, j, r):
        target = (grad_k, grad_v)[kind].at[0, :, kv_columns(core, j)]
        if r is core:
            return pltpu.make_async_copy(kv_stage.at[j, kind, r], target, kv_sem.at[j, kind])
        return remote(
            kv_stage.at[j, kind, r], target, kv_send.at[j, kind], kv_recv.at[j, kind], sibling
        )

    other = 1 - core

    def reduce_last(j):
        add_sum(j, 1, 4)
        slot = at_slot(SLOTS - 1)
        d_key = acc[j, 0, :, slot].T
        d_value = acc[j, 1, :, slot].T
        k_unit, k_inverse = unit_rows(kv_raw[j, 0, slot, :])
        scaled = d_key * gain_k
        result = (
            scaled - k_unit * jnp.mean(scaled * k_unit, axis=-1, keepdims=True)
        ) * k_inverse
        kv_stage[j, 0] = result.astype(BF16).reshape(2, ROWS, HEAD_DIM)
        kv_stage[j, 1] = d_value.astype(BF16).reshape(2, ROWS, HEAD_DIM)
        for kind in range(2):
            kv_copy(kind, j, other).start()
            kv_copy(kind, j, core).start()

    def out_copy(kind, j, r):
        target = (attended, grad_q)[kind].at[0, :, q_columns(core, j)]
        source = out_stage.at[kind, r, :, pl.ds(pl.multiple_of(j * 1024, 1024), 1024)]
        if r is core:
            return pltpu.make_async_copy(source, target, out_sem.at[kind, j])
        return remote(source, target, out_send.at[kind, j], out_recv.at[kind, j], sibling)

    def attend(j, r):
        columns = [
            pl.ds(pl.multiple_of((j * GROUP + head) * HEAD_DIM, HEAD_DIM), HEAD_DIM)
            for head in range(GROUP)
        ]
        q_unit, q_inverse = unit_rows(jnp.concatenate([q_raw[r, :, at] for at in columns], 0))
        q = (q_unit * gain_q).astype(BF16)
        up = jnp.concatenate([up_raw[r, :, at] for at in columns], 0)
        seen = pl.ds(pl.multiple_of(r * ROWS, ROWS), SEEN)
        k = k_normed[j, seen, :]
        v = kv_raw[j, 1, seen, :]
        scores = matmul(q, k, 1, 1)
        d_probs = matmul(up, v, 1, 1)
        scores = (scores.reshape(GROUP, ROWS, SEEN) + bias[r][None]).reshape(GROUP * ROWS, SEEN)
        top = jnp.max(scores, axis=1, keepdims=True)
        weights = jnp.exp2((scores - top) * EXP2_FACTOR)
        probs = weights * (1.0 / jnp.sum(weights, axis=1, keepdims=True))
        probs_b = probs.astype(BF16)
        out = matmul(probs_b, v, 1, 0).astype(BF16)
        delta = jnp.sum(up.astype(F32) * out.astype(F32), axis=1, keepdims=True)
        d_scores = (probs * (d_probs - delta) * FACTOR).astype(BF16)
        d_qn = matmul(d_scores, k, 1, 0).astype(BF16).astype(F32)
        acc[j, 0, :, seen] += matmul(q, d_scores, 0, 0)
        acc[j, 1, :, seen] += matmul(up, probs_b, 0, 0)
        gain_acc[0] += jnp.sum((d_qn * q_unit).reshape(ROWS, GROUP, HEAD_DIM), axis=0)
        scaled = d_qn * gain_q
        d_query = (
            (scaled - q_unit * jnp.mean(scaled * q_unit, axis=-1, keepdims=True)) * q_inverse
        ).astype(BF16)
        for head, at in enumerate(columns):
            rows = slice(head * ROWS, (head + 1) * ROWS)
            out_stage[0, r, :, at] = out[rows]
            out_stage[1, r, :, at] = d_query[rows]

    def prepare(j):
        gather_copy(j, 2).wait_recv()
        gather_copy(j, 3).wait_recv()
        unit, _ = unit_rows(kv_raw[j, 0])
        k_normed[j] = (unit * gain_k).astype(BF16)
        k_unit_t[j] = unit.T

    def finish(j):
        product = acc[j, 0] * k_unit_t[j]
        total = product[:, :128]
        for piece in range(1, SPAN // 128):
            total = total + product[:, piece * 128 : (piece + 1) * 128]
        gain_acc[1] += jnp.sum(total.T.reshape(16, 8, HEAD_DIM), axis=0)

    def step(i, carry):
        j = i // 2

        @pl.when(i % 2 == 0)
        def _():
            for half in range(2):

                @pl.when(j == half)
                def _():
                    prepare(half)
                    for kind in range(2, 4):
                        core_copy(kind, half).wait_recv()

        @pl.when(i % 2 == 1)
        def _():
            for half in range(2):

                @pl.when(j == half)
                def _():
                    for kind in range(2, 4):
                        own_copy(kind, half).wait()

        attend(j, jnp.where(i % 2 == 0, other, core))

        @pl.when(i == 0)
        def _():
            for kind in range(2):
                out_copy(kind, 0, other).start()

        @pl.when(i == 1)
        def _():
            for kind in range(2):
                out_copy(kind, 0, core).start()
            finish(0)
            reduce_first(0)

        @pl.when(i == 2)
        def _():
            for kind in range(2):
                out_copy(kind, 1, other).start()
            reduce_second(0)

        @pl.when(i == 3)
        def _():
            for kind in range(2):
                out_copy(kind, 1, core).start()
            finish(1)
            reduce_first(1)

        return carry

    lax.fori_loop(0, 4, step, 0)

    def gain_a_copy(step):
        return remote(
            gain_a.at[0], gain_a.at[step], ga_send.at[step], ga_recv.at[step], z_peer(step)
        )

    def gain_b_copy(code):
        return remote(
            gain_b.at[0], gain_b.at[code], gb_send.at[code], gb_recv.at[code], square_peer(code)
        )

    gain_a[0, 0:1] = jnp.sum(gain_acc[0], axis=0, keepdims=True)
    gain_a[0, 1:2] = jnp.sum(gain_acc[1], axis=0, keepdims=True)
    gain_a[0, 2:8] = jnp.zeros((6, HEAD_DIM), F32)
    for at in range(1, 8):
        gain_a_copy(at).start()
    reduce_third(0)
    reduce_second(1)
    for at in range(1, 8):
        gain_a_copy(at).wait_recv()
    terms = gain_a[z % 8]
    for at in range(1, 8):
        terms = terms + gain_a[(z + 8 - at) % 8]
    gain_b[0] = terms
    for at in range(1, 8):
        gain_b_copy(at).start()
    reduce_last(0)
    reduce_third(1)
    reduce_last(1)
    for at in range(1, 8):
        gain_b_copy(at).wait_recv()
    sums = []
    for m in range(2):
        total = None
        for h in range(2):
            for c in range(2):
                term = gain_b[((mirror + m) % 2) * 4 + ((col + h) % 2) * 2 + (core + c) % 2]
                total = term if total is None else total + term
        sums.append(total)
    result = sums[0] + sums[1]
    grad_gains[:, :HEAD_DIM] = result[0:1]
    grad_gains[:, HEAD_DIM:] = result[1:2]

    for j in range(2):
        for kind in range(4):
            core_copy(kind, j).wait_send()
        for at in range(4):
            gather_copy(j, at).wait_send()
            reduce_copy(j, at).wait_send()
        for kind in range(2):
            out_copy(kind, j, core).wait()
            out_copy(kind, j, other).wait()
            kv_copy(kind, j, core).wait()
            kv_copy(kind, j, other).wait()
    for at in range(1, 8):
        gain_a_copy(at).wait_send()
        gain_b_copy(at).wait_send()


def on_device(queries, key_rows, value_rows, upstream, norm_gains, segments):
    any_space = pl.BlockSpec(memory_space=pl.ANY)
    vmem = pl.BlockSpec(memory_space=pltpu.VMEM)
    dma = pltpu.SemaphoreType.DMA
    return tuple(
        pl.pallas_call(
            kernel,
            out_shape=[
                jax.ShapeDtypeStruct(queries.shape, BF16),
                jax.ShapeDtypeStruct(queries.shape, BF16),
                jax.ShapeDtypeStruct(key_rows.shape, BF16),
                jax.ShapeDtypeStruct(key_rows.shape, BF16),
                jax.ShapeDtypeStruct(norm_gains.shape, F32),
            ],
            in_specs=[any_space] * 4 + [vmem] * 2,
            out_specs=[any_space] * 4 + [vmem],
            scratch_shapes=[
                pltpu.VMEM((2, ROWS, 2048), BF16),
                pltpu.VMEM((2, ROWS, 2048), BF16),
                pltpu.VMEM((2, 2, SPAN, HEAD_DIM), BF16),
                pltpu.VMEM((2, SPAN, HEAD_DIM), BF16),
                pltpu.VMEM((2, HEAD_DIM, SPAN), F32),
                pltpu.VMEM((2, ROWS, SEEN), F32),
                pltpu.VMEM((2, 2, HEAD_DIM, SPAN), F32),
                pltpu.VMEM((2, 2, ROWS, 2048), BF16),
                pltpu.VMEM((2, 2, 2, ROWS, HEAD_DIM), BF16),
                pltpu.VMEM((2, 2, 2, HEAD_DIM, PAIR), BF16),
                pltpu.VMEM((2, 2, 2, HEAD_DIM, PAIR), BF16),
                pltpu.VMEM((2, 2, 2, HEAD_DIM, PAIR), BF16),
                pltpu.VMEM((2, 2, 2, HEAD_DIM, PAIR), BF16),
                pltpu.VMEM((2, 8, HEAD_DIM), F32),
                pltpu.VMEM((8, 8, HEAD_DIM), F32),
                pltpu.VMEM((8, 8, HEAD_DIM), F32),
                dma((4, 2)),
                dma((4, 2)),
                dma((4, 2)),
                dma((2, 4)),
                dma((2, 4)),
                dma((2, 4)),
                dma((2, 4)),
                dma((2, 2)),
                dma((2, 2)),
                dma((2, 2)),
                dma((2, 2)),
                dma((2, 2)),
                dma((2, 2)),
                dma((8,)),
                dma((8,)),
                dma((8,)),
                dma((8,)),
            ],
            compiler_params=pltpu.CompilerParams(
                collective_id=0, has_side_effects=True, vmem_limit_bytes=56 * 2**20
            ),
            cost_estimate=pl.CostEstimate(
                flops=6 * 10**9, bytes_accessed=5 * 10**6, transcendentals=5 * 10**6
            ),
        )(queries, key_rows, value_rows, upstream, norm_gains, segments)
    )


def solution(mesh):
    rows = P("section", "seq", None)
    whole = P("section", None)
    return jax.shard_map(
        on_device,
        mesh=mesh,
        in_specs=(rows, rows, rows, rows, whole, whole),
        out_specs=(rows, rows, rows, rows, whole),
        check_vma=False,
    )
```

time: 404 us -> 72 us (0.18); the launches traced: 397 us -> 71.8 us
  waiting for transfers between devices: 144 us -> 0 us
  blocking collectives: 75.4 us -> 0 us
  Pallas kernels: 0 us -> 65.6 us
  starting transfers between devices: 59 us -> 0 us
  local copies, waits for them, and re-layouts: 51.6 us -> 5.58 us
  matrix products: 39.9 us -> 0 us
  other arithmetic: 25 us -> 0 us
    all_to_all x8 -> x0, waiting for transfers between devices: 142 us -> none  [the longest x1 28 us: on_device(): lax.all_to_all(k_copies, 'seq', split_axis=1, concat_axis=0, tiled=True)]
    psum x1 -> x0, blocking collectives: 75.4 us -> none  [on_device(): group_terms = lax.psum(local_terms, 'seq')]
    pallas_call x0 -> x1, Pallas kernels: none -> 65.6 us  [on_device(): pl.pallas_call(kernel, out_shape=[jax.ShapeDtypeStruct(queries.shape, BF1...]
    all_to_all x8 -> x0, starting transfers between devices: 54.9 us -> none  [the longest x1 12.8 us: on_device(): lax.all_to_all(k_copies, 'seq', split_axis=1, concat_axis=0, tiled=True)]
    dot_general x48 -> x0, matrix products: 39.9 us -> none  [the longest x8 9.42 us: attend_head(): dk_part = jnp.dot(d_scores.T, q_block, preferred_element_type=jnp.float32)]
    slice x22 -> x0, local copies, waits for them, and re-layouts: 23.5 us -> none  [the longest x9 12.7 us: attend_head(): q_block = q_head[first:last]]
    reduce_sum x21 -> x0, other arithmetic: 13.1 us -> none  [the longest x8 3.95 us: attend_head(): probs = weights / jnp.sum(weights, axis=1, keepdims=True)]
    unnamed x184 -> x13, local copies, waits for them, and re-layouts: 16.7 us -> 5.58 us
  transfers between devices with their start and end apart: 11 -> 0, of which waited for: 8 -> 0; matrix products, arithmetic and copies ran while one was open for 16% -> 0% of each run, Pallas kernels for 0% -> 0%
where the time goes in v1:
time: 72 us; the launch traced here: 71.8 us
  Pallas kernels  65.6 us (91%)
  local copies, waits for them, and re-layouts  5.58 us (8%)
    pallas_call x1, Pallas kernels, on_device(): pl.pallas_call(kernel, out_shape=[jax.ShapeDtypeStruct(queries.shape, BF1...  65.6 us
    unnamed x13, local copies, waits for them, and re-layouts  5.58 us

profile of v1, /device:TPU:1, one launch (start us, length us, event | category | flops | bytes accessed | tf_op | source)
XLA Modules:
  0.0 71.8 jit_solution(6052222326255470955)
XLA Ops:
  0.6 65.6 %shard_map.101 = (bf16[1,128,4096]{2,1,0:T(8,128)(2,1)}, bf16[1,128,4096]{2,1,0:T(8,128)(2,1)}, bf16[1,128,512]{2,1,0:T(8,128)(2,1)}, bf16[1,128,512]{2,1,0:T(8,128)(2,1)}, f32[1,256]{1,0:T(1,128)}) custom-call(bf16[1,128,4096]{2,1,0:T(8,128)(2,1)} %queries.1, bf16[1,128,512]{2,1,0:T(8,128)(2,1)} %keys.1, bf16[1,128,512]{2,1,0:T(8,128)(2,1)} %values.1, ...), custom_call_target="tpu_custom_call" | custom-call | flops 6000000000 | bytes 5000000 | tf_op jit(solution)/shard_map/pallas_call | solution.py:453
  66.2 0.0 copy-start
  66.2 2.4 %copy.16 = bf16[1,128,4096]{2,1,0:T(8,128)(2,1)} copy(bf16[1,128,4096]{2,1,0:T(8,128)(2,1)} %get-tuple-element.10) | data formatting | bytes 2097152
  68.6 0.0 copy-done
  68.6 0.0 copy-start.2
  68.6 1.0 %copy.17 = bf16[1,128,4096]{2,1,0:T(8,128)(2,1)} copy(bf16[1,128,4096]{2,1,0:T(8,128)(2,1)S(1)} %copy-done) | data formatting | bytes 2097152
  69.6 0.1 copy-done.2
  69.6 0.0 copy-start.1
  69.6 0.7 copy.18
  70.3 0.3 copy-done.1
  70.6 0.0 copy-start.3
  70.6 0.7 copy.19
  71.2 0.0 copy-done.3
  71.2 0.6 copy.20
Async XLA Ops:
  66.2 2.4 %copy-start = (bf16[1,128,4096]{2,1,0:T(8,128)(2,1)S(1)}, bf16[1,128,4096]{2,1,0:T(8,128)(2,1)}, u32[]{:S(2)}) copy-start(bf16[1,128,4096]{2,1,0:T(8,128)(2,1)} %get-tuple-element.11) | copy-start | bytes 3145732
  68.6 1.0 %copy-start.2 = (bf16[1,128,512]{2,1,0:T(8,128)(2,1)S(1)}, bf16[1,128,512]{2,1,0:T(8,128)(2,1)}, u32[]{:S(2)}) copy-start(bf16[1,128,512]{2,1,0:T(8,128)(2,1)} %get-tuple-element.12) | copy-start | bytes 393220
  69.6 1.0 %copy-start.1 = (bf16[1,128,512]{2,1,0:T(8,128)(2,1)S(1)}, bf16[1,128,512]{2,1,0:T(8,128)(2,1)}, u32[]{:S(2)}) copy-start(bf16[1,128,512]{2,1,0:T(8,128)(2,1)} %get-tuple-element.13) | copy-start | bytes 393220
  70.6 0.7 copy-start.3
